TPU v7x, 768 devices: a whole 4x8x12 slice. The times are simulated.
768 devices in a mesh: row: 4 (over z_hi, core), col: 24 (over x, z_lo), ri: 8 (over y).
Axes of the slice: x: 4, y: 8, z: 12 (z_hi: 2, z_lo: 6; z = z_hi * 6 + z_lo), core: 2. Of those that a mesh axis runs over, the one named last changes fastest.
Arguments:
- coulomb3: bfloat16 [768, 768, 768], P(('row', 'ri'), 'col'), may hold values from -6 to 6
- tile_mask: int32 [24, 24], replicated, may hold values from 0 to 1, as said below
- tile_fill: int32 [24], replicated, may hold values from 16 to 32, as said below
- occ_density: bfloat16 [768, 768], P('col'), may hold values from -0.21875 to 0.21875
- virt_density: bfloat16 [768, 768], P('col'), may hold values from -0.21875 to 0.21875
Outputs:
- transformed: bfloat16 [32, 24, 768, 768], P(('row', 'ri'), 'col')
Inputs may be any that keep to these rules, and one draw needn't show every extreme that they name: tile_mask[a, b] is 1 where atom blocks a and b pass screening; it is symmetric and 1 on the diagonal. tile_fill[t] counts the basis functions of tile t, which occupy its first positions; the rest is padding. Some tile is full and some tile holds exactly 16.
All inputs are finite; a program needn't handle non-finite values.
Results may differ from a plain program's by a relative error of at most 0.0049.
Values may be sent and summed in bfloat16 or wider, within the bound.
A program may use at most 32 MiB of HBM per device.

v0:
```python
import jax
import jax.numpy as jnp
from jax import lax
from jax.sharding import PartitionSpec as P


def tile_weights(tile_mask, tile_fill, norb, mu_dev, col_place):
    tiles = tile_fill.shape[0]
    tile_width = norb // tiles
    positions = jnp.arange(norb, dtype=jnp.int32)
    onehot = (
        positions[:, None] // tile_width == jnp.arange(tiles, dtype=jnp.int32)[None, :]
    ).astype(jnp.int32)
    capacity = jnp.sum(onehot * tile_fill[None, :], axis=1)
    live = (positions % tile_width < capacity).astype(jnp.int32)
    own_onehot = lax.dynamic_slice_in_dim(onehot, col_place * mu_dev, mu_dev, 0)
    own_live = lax.dynamic_slice_in_dim(live, col_place * mu_dev, mu_dev, 0)
    pair = jnp.dot(jnp.dot(own_onehot, tile_mask), onehot.T)
    weight = (pair * own_live[:, None] * live[None, :]).astype(jnp.bfloat16)
    return (weight, live.astype(jnp.float32))


def on_device(coulomb3, tile_mask, tile_fill, occ_density, virt_density):
    p_dev, mu_dev, norb = coulomb3.shape
    weight, live_float = tile_weights(tile_mask, tile_fill, norb, mu_dev, lax.axis_index("col"))
    screened = coulomb3 * weight[None]
    half_trans = jnp.einsum(
        "pmn,ns->pms",
        screened,
        lax.all_gather(occ_density, "col", axis=0, tiled=True),
        preferred_element_type=jnp.float32,
    ).astype(jnp.bfloat16)
    moved = lax.all_to_all(half_trans, "col", split_axis=0, concat_axis=1, tiled=True)
    product = jnp.einsum(
        "lm,pms->pls",
        lax.all_gather(virt_density, "col", axis=0, tiled=True),
        moved,
        preferred_element_type=jnp.float32,
    )
    result = (product * live_float[None, :, None] * live_float[None, None, :]).astype(jnp.bfloat16)
    return result[None]


def solution(mesh):
    placed = (P(("row", "ri"), "col", None), P(), P(), P("col", None), P("col", None))
    return jax.shard_map(
        on_device,
        mesh=mesh,
        in_specs=placed,
        out_specs=P(("row", "ri"), "col", None, None),
        check_vma=False,
    )
```

profile of v0, /device:TPU:8, one launch (start us, length us, event | category | flops | bytes accessed | tf_op | source)
XLA Modules:
  0.0 354.5 jit_solution(5129408108801740314)
XLA Ops:
  6.5 0.0 copy-start
  6.5 0.0 all-gather.3.cloned.1.call-start
  6.5 0.7 all-gather.3.cloned.1.call-update
  7.3 0.7 select_reduce_fusion
  8.0 0.1 dynamic_slice.7
  8.1 0.0 copy-done
  8.1 0.5 fusion.6
  8.6 166.7 %all-gather.3.cloned.1.call-done = bf16[768,768]{1,0:T(8,128)(2,1)} async-done(((bf16[32,768]{1,0:T(8,128)(2,1)}), bf16[768,768]{1,0:T(8,128)(2,1)}) %all-gather.3.cloned.1.call-update) | async-done | bytes 1179664 | tf_op jit(solution)/shard_map/all_gather | solution.py:30
  175.3 3.7 %convolution_convert_fusion = bf16[24,32,768]{2,1,0:T(8,128)(2,1)} fusion(bf16[768,768]{1,0:T(8,128)(2,1)} %all-gather.3.cloned.1.call-done, bf16[24,32,768]{2,1,0:T(8,128)(2,1)} %param.5, bf16[32,768]{1,0:T(8,128)(2,1)S(1)} %fusion.6), kind=kOutput, calls=%fused_computation.3 | convolution fusion | flops 907149312 | bytes 3588096 | tf_op jit(solution)/shard_map/pmn,ns->pms/dot_general | solution.py:27
  179.0 3.9 %all-to-all-start = ((bf16[24,32,768]{2,1,0:T(8,128)(2,1)}), bf16[24,32,768]{2,1,0:T(8,128)(2,1)S(1)}, u32[]{:S(2)}, u32[]{:S(2)}) async-start(bf16[24,32,768]{2,1,0:T(8,128)(2,1)} %convolution_convert_fusion), calls=%async_computation | async-start | bytes 2359296 | tf_op jit(solution)/shard_map/all_to_all | solution.py:33
  183.0 0.0 all-gather.5.cloned.1.call-start
  183.0 0.7 all-gather.5.cloned.1.call-update
  183.7 159.9 %all-gather.5.cloned.1.call-done = bf16[768,768]{1,0:T(8,128)(2,1)} async-done(((bf16[32,768]{1,0:T(8,128)(2,1)}), bf16[768,768]{1,0:T(8,128)(2,1)}) %all-gather.5.cloned.1.call-update) | async-done | bytes 1179664 | tf_op jit(solution)/shard_map/all_gather | solution.py:36
  343.7 0.0 all-to-all-done
  343.7 2.5 fusion.2
  346.2 1.5 copy.7
  (3 shorter events, 0.0 us)
Async XLA Ops:
  6.5 1.6 copy-start
  6.5 168.8 %all-gather.3.cloned.1.call-start = ((), (), s32[]{:S(2)}) async-start(), calls=%async_computation.1 | async-start | bytes 1228800 | tf_op jit(solution)/shard_map/all_gather | solution.py:30
  179.0 164.6 %all-to-all-start = ((bf16[24,32,768]{2,1,0:T(8,128)(2,1)}), bf16[24,32,768]{2,1,0:T(8,128)(2,1)S(1)}, u32[]{:S(2)}, u32[]{:S(2)}) async-start(bf16[24,32,768]{2,1,0:T(8,128)(2,1)} %convolution_convert_fusion), calls=%async_computation | async-start | bytes 2359296 | tf_op jit(solution)/shard_map/all_to_all | solution.py:33
  183.0 160.7 %all-gather.5.cloned.1.call-start = ((), (), s32[]{:S(2)}) async-start(), calls=%async_computation.2 | async-start | bytes 1228800 | tf_op jit(solution)/shard_map/all_gather | solution.py:36
Sparse Core Ops, SparseCore 0:
  9.7 165.5 all-gather.2
  186.2 157.4 all-gather.4
where the time goes:
time: 355 us; the launch traced here: 354 us
  waiting for transfers between devices  328 us (92%)
  between operations  13.5 us (4%)
  matrix products  6.7 us (2%)
  starting transfers between devices  3.98 us (1%)
    all_gather x1, waiting for transfers between devices, on_device(): lax.all_gather(occ_density, 'col', axis=0, tiled=True)  167 us
    all_gather x1, waiting for transfers between devices, on_device(): lax.all_gather(virt_density, 'col', axis=0, tiled=True)  160 us
  transfers between devices with their start and end apart: 3, of which 2 were waited for; matrix products, arithmetic and copies ran while one was open for 0% of the time, Pallas kernels for 0%

commit v1 on v0

v1 whole, which is shorter than its diff:
```python
import functools

import jax
import jax.numpy as jnp
from jax import lax
from jax.experimental import pallas as pl
from jax.experimental.pallas import tpu as pltpu
from jax.sharding import PartitionSpec as P

MESH = pl.DeviceIdType.MESH
NX, NZ, NY = 4, 6, 8
BS, NTILE, NORB = 32, 24, 768
SLABS = NORB // 128
GROUP = NZ * BS


def gather_kernel(
    width, fill_ref, mask_ref, c_hbm, o_hbm, v_hbm, h_ref, vm_ref,
    c_in, c_out, c_got, own, full, pick, occ,
    load_sem, send_sem, recv_sem, z_send, z_recv, y_send, y_recv, x_send, x_recv, k_send, k_recv,
):
    row, col, y = lax.axis_index("row"), lax.axis_index("col"), lax.axis_index("ri")
    x, z = col // NZ, col % NZ
    core = row % 2
    other = row + 1 - 2 * core

    loads = [
        pltpu.make_async_copy(o_hbm, own.at[0], load_sem.at[0]),
        pltpu.make_async_copy(v_hbm, own.at[1], load_sem.at[1]),
        pltpu.make_async_copy(c_hbm, c_in, load_sem.at[2]),
    ]
    for load in loads:
        load.start()

    barrier = pltpu.get_barrier_semaphore()

    def greet_col(d, _):
        pl.semaphore_signal(barrier, inc=1, device_id={"col": (col + d) % NTILE}, device_id_type=MESH)
        return 0

    def greet_y(d, _):
        pl.semaphore_signal(barrier, inc=1, device_id={"ri": (y + d) % NY}, device_id_type=MESH)
        return 0

    lax.fori_loop(1, NTILE, greet_col, 0)
    lax.fori_loop(1, NY, greet_y, 0)
    pl.semaphore_signal(barrier, inc=1, device_id={"row": other}, device_id_type=MESH)

    place = lax.broadcasted_iota(jnp.int32, (8, NORB), 1)
    tile, pos = place // BS, place % BS
    rank = jnp.full((8, NORB), -1, jnp.int32)
    weight = jnp.zeros((8, NORB), jnp.int32)
    offset = jnp.int32(0)
    for t in range(NTILE):
        here = (tile == t) & (pos < fill_ref[t])
        rank = jnp.where(here, pos + offset, rank)
        weight = jnp.where(here, mask_ref[col, t], weight)
        offset = offset + fill_ref[t]
    live = (rank >= 0).astype(jnp.float32)[:1]
    weight = weight.astype(jnp.float32)[:1]

    def build(i, _):
        rows = pl.ds(i * 128, 128)
        want = lax.broadcasted_iota(jnp.int32, (128, NORB), 0) + i * 128
        pick[rows, :] = (rank[:1] == want).astype(jnp.float32).astype(jnp.bfloat16)
        return 0

    lax.fori_loop(0, width // 128, build, 0)

    live_rows = lax.broadcasted_iota(jnp.int32, (BS, 1), 0) < fill_ref[col]
    screen = (weight * live_rows.astype(jnp.float32)).astype(jnp.bfloat16)
    loads[2].wait()

    def pack(i, _):
        block = (c_in[:, i] * screen[None]).reshape(NX * BS, NORB)
        packed = lax.dot_general(block, pick[...], (((1,), (1,)), ((), ())), preferred_element_type=jnp.float32)
        c_out[i] = packed.astype(jnp.bfloat16).reshape(NX, BS, width)
        return 0

    lax.fori_loop(0, NZ, pack, 0)
    loads[0].wait()
    loads[1].wait()
    pl.semaphore_wait(barrier, NTILE + NY - 1)

    def z_copy(to, at):
        rows = pl.ds(x * GROUP + at * BS, BS)
        cols = pl.ds(pl.multiple_of(y * 128, 128), 128)
        return pltpu.make_async_remote_copy(
            src_ref=own.at[core, :, cols], dst_ref=full.at[core, rows, cols],
            send_sem=z_send.at[to], recv_sem=z_recv.at[at],
            device_id={"col": x * NZ + to}, device_id_type=MESH,
        )

    def own_z():
        cols = pl.ds(pl.multiple_of(y * 128, 128), 128)
        return pltpu.make_async_copy(own.at[core, :, cols], full.at[core, pl.ds(col * BS, BS), cols], load_sem.at[0])

    def y_copy(to, at):
        rows = pl.ds(x * GROUP, GROUP)
        cols = pl.ds(pl.multiple_of(at * 128, 128), 128)
        return pltpu.make_async_remote_copy(
            src_ref=full.at[core, rows, cols], dst_ref=full.at[core, rows, cols],
            send_sem=y_send.at[to], recv_sem=y_recv.at[at],
            device_id={"ri": to}, device_id_type=MESH,
        )

    def x_copy(to, at):
        rows = pl.ds(at * GROUP, GROUP)
        return pltpu.make_async_remote_copy(
            src_ref=full.at[core, rows], dst_ref=full.at[core, rows],
            send_sem=x_send.at[to], recv_sem=x_recv.at[at],
            device_id={"col": to * NZ + z}, device_id_type=MESH,
        )

    def k_copy(part, at):
        rows = pl.ds(part * GROUP, GROUP)
        return pltpu.make_async_remote_copy(
            src_ref=full.at[at, rows], dst_ref=full.at[at, rows],
            send_sem=k_send.at[part], recv_sem=k_recv.at[part],
            device_id={"row": other}, device_id_type=MESH,
        )

    def c_copy(to_x, to_z, at_x, at_z):
        return pltpu.make_async_remote_copy(
            src_ref=c_out.at[to_z, to_x], dst_ref=c_got.at[at_z, at_x],
            send_sem=send_sem.at[to_z, to_x], recv_sem=recv_sem.at[at_z, at_x],
            device_id={"col": to_x * NZ + to_z}, device_id_type=MESH,
        )

    @pl.when(y < SLABS)
    def _():
        def send(d, _):
            z_copy((z + d) % NZ, z).start()
            return 0

        own_z().start()
        lax.fori_loop(1, NZ, send, 0)

    half = z // 3
    keep = pltpu.make_async_copy(c_out.at[z, x], c_got.at[z, x], load_sem.at[2])
    keep.start()

    def send_tile(i, _):
        to_z = (i + 3 * (1 - half)) % NZ

        def send(d, _):
            to_x = (x + d) % NX

            @pl.when((d > 0) | (to_z != z))
            def _():
                c_copy(to_x, to_z, x, z).start()

            return 0

        return lax.fori_loop(0, NX, send, 0)

    lax.fori_loop(0, NZ, send_tile, 0)

    @pl.when(y < SLABS)
    def _():
        def take(d, _):
            z_copy(z, (z + d) % NZ).wait_recv()
            return 0

        def send(d, _):
            y_copy((y + d) % NY, y).start()
            return 0

        own_z().wait()
        lax.fori_loop(1, NZ, take, 0)
        lax.fori_loop(1, NY, send, 0)

    def take_y(s, _):
        @pl.when(y != s)
        def _():
            y_copy(y, s).wait_recv()

        return 0

    lax.fori_loop(0, SLABS, take_y, 0)

    def send_x(d, _):
        x_copy((x + d) % NX, x).start()
        return 0

    lax.fori_loop(1, NX, send_x, 0)
    k_copy(x, core).start()

    def take_x(d, _):
        part = (x + d) % NX
        x_copy(x, part).wait_recv()
        k_copy(part, core).start()
        return 0

    lax.fori_loop(1, NX, take_x, 0)

    def take_k(part, _):
        k_copy(part, 1 - core).wait_recv()
        return 0

    lax.fori_loop(0, NX, take_k, 0)

    def pack_occ(i, _):
        rows = pl.ds(i * 128, 128)
        packed = jnp.dot(pick[rows, :], full[0], preferred_element_type=jnp.float32)
        occ[rows, :] = (packed * live).astype(jnp.bfloat16)
        return 0

    lax.fori_loop(0, width // 128, pack_occ, 0)

    for t in range(NTILE):
        rows = pl.ds(t * BS, BS)
        alive = lax.broadcasted_iota(jnp.int32, (BS, NORB), 0) < fill_ref[t]
        vm_ref[rows, :] = jnp.where(alive, full[1, rows, :].astype(jnp.float32), 0.0).astype(jnp.bfloat16)

    keep.wait()

    def transform(i, _):
        at_z = (i + 3 * half) % NZ

        def take(d, _):
            at_x = (x + d) % NX

            @pl.when((d > 0) | (at_z != z))
            def _():
                c_copy(x, z, at_x, at_z).wait_recv()

            return 0

        lax.fori_loop(0, NX, take, 0)
        got = c_got[at_z].reshape(NX * BS, width)
        done = jnp.dot(got, occ[...], preferred_element_type=jnp.float32).astype(jnp.bfloat16)
        for k in range(NX):
            h_ref[pl.ds(k * GROUP + at_z * BS, BS), :] = done[k * BS:(k + 1) * BS]
        return 0

    lax.fori_loop(0, NZ, transform, 0)

    @pl.when(y < SLABS)
    def _():
        def left_z(d, _):
            z_copy((z + d) % NZ, z).wait_send()
            return 0

        def left_y(d, _):
            y_copy((y + d) % NY, y).wait_send()
            return 0

        lax.fori_loop(1, NZ, left_z, 0)
        lax.fori_loop(1, NY, left_y, 0)

    def left_x(d, _):
        x_copy((x + d) % NX, x).wait_send()
        return 0

    def left_k(part, _):
        k_copy(part, core).wait_send()
        return 0

    def left_c(i, _):
        to_z, to_x = i // NX, i % NX

        @pl.when((to_z != z) | (to_x != x))
        def _():
            c_copy(to_x, to_z, x, z).wait_send()

        return 0

    lax.fori_loop(1, NX, left_x, 0)
    lax.fori_loop(0, NX, left_k, 0)
    lax.fori_loop(0, NTILE, left_c, 0)


def gather(width, coulomb3, tile_mask, tile_fill, occ_density, virt_density):
    dma = pltpu.SemaphoreType.DMA
    bf16 = jnp.bfloat16
    return pl.pallas_call(
        functools.partial(gather_kernel, width),
        out_shape=[jax.ShapeDtypeStruct((NORB, NORB), bf16)] * 2,
        in_specs=[pl.BlockSpec(memory_space=pltpu.SMEM)] * 2 + [pl.BlockSpec(memory_space=pl.ANY)] * 3,
        out_specs=[pl.BlockSpec(memory_space=pltpu.VMEM)] * 2,
        scratch_shapes=[
            pltpu.VMEM((NX, NZ, BS, NORB), bf16),
            pltpu.VMEM((NZ, NX, BS, width), bf16),
            pltpu.VMEM((NZ, NX, BS, width), bf16),
            pltpu.VMEM((2, BS, NORB), bf16),
            pltpu.VMEM((2, NORB, NORB), bf16),
            pltpu.VMEM((width, NORB), bf16),
            pltpu.VMEM((width, NORB), bf16),
            dma((3,)), dma((NZ, NX)), dma((NZ, NX)), dma((NZ,)), dma((NZ,)),
            dma((NY,)), dma((NY,)), dma((NX,)), dma((NX,)), dma((NX,)), dma((NX,)),
        ],
        compiler_params=pltpu.CompilerParams(
            collective_id=width // 64, has_side_effects=True, vmem_limit_bytes=40 * 1024 * 1024
        ),
        name=f"gather_{width}",
    )(tile_fill, tile_mask, coulomb3.reshape(NX, NZ, BS, NORB), occ_density, virt_density)


def second_kernel(v_ref, h_ref, out_ref):
    out_ref[...] = jnp.dot(v_ref[...], h_ref[...], preferred_element_type=jnp.float32).astype(jnp.bfloat16)


def second(virt, half_trans):
    rows = 256
    return pl.pallas_call(
        second_kernel,
        out_shape=jax.ShapeDtypeStruct((NORB, NORB), jnp.bfloat16),
        grid=(NORB // rows,),
        in_specs=[pl.BlockSpec((rows, NORB), lambda i: (i, 0)), pl.BlockSpec((NORB, NORB), lambda i: (0, 0))],
        out_specs=pl.BlockSpec((rows, NORB), lambda i: (i, 0)),
        name="second",
    )(virt, half_trans)


def on_device(coulomb3, tile_mask, tile_fill, occ_density, virt_density):
    half_trans, virt = gather(NORB, coulomb3, tile_mask, tile_fill, occ_density, virt_density)
    return second(virt, half_trans)[None, None]


def solution(mesh):
    placed = (P(("row", "ri"), "col", None), P(), P(), P("col", None), P("col", None))
    return jax.shard_map(
        on_device,
        mesh=mesh,
        in_specs=placed,
        out_specs=P(("row", "ri"), "col", None, None),
        check_vma=False,
    )
```

time: 355 us -> 77 us (0.22)
  the two profiles are of different devices: /device:TPU:8 before, /device:TPU:133 now
where the time goes in v1:
time: 77 us; the launch traced here: 76.6 us
  Pallas kernels  70.3 us (91%)
  local copies, waits for them, and re-layouts  6.27 us (8%)
    pallas_call x1, Pallas kernels, gather(): pl.pallas_call(functools.partial(gather_kernel, width), out_shape=[jax.Sh...  66.1 us
    unnamed x14, local copies, waits for them, and re-layouts  6.27 us
    pallas_call x1, Pallas kernels, second(): pl.pallas_call(second_kernel, out_shape=jax.ShapeDtypeStruct((NORB, NORB)...  4.25 us

profile of v1, /device:TPU:133, one launch (start us, length us, event | category | flops | bytes accessed | tf_op | source)
XLA Modules:
  0.0 76.6 jit_solution(5533553292302457009)
XLA Ops:
  0.0 0.0 copy-start.2
  0.0 1.3 %copy-done.2 = bf16[24,32,768]{2,1,0:T(8,128)(2,1)S(1)} copy-done((bf16[24,32,768]{2,1,0:T(8,128)(2,1)S(1)}, bf16[24,32,768]{2,1,0:T(8,128)(2,1)}, u32[]{:S(2)}) %copy-start.2) | copy-done | bytes 1179672
  1.3 0.0 copy-start.3
  1.3 0.8 %copy-done.3 = bf16[32,768]{1,0:T(8,128)(2,1)S(1)} copy-done((bf16[32,768]{1,0:T(8,128)(2,1)S(1)}, bf16[32,768]{1,0:T(8,128)(2,1)}, u32[]{:S(2)}) %copy-start.3) | copy-done | bytes 49176
  2.1 0.0 copy-start.4
  2.1 0.8 %copy-done.4 = bf16[32,768]{1,0:T(8,128)(2,1)S(1)} copy-done((bf16[32,768]{1,0:T(8,128)(2,1)S(1)}, bf16[32,768]{1,0:T(8,128)(2,1)}, u32[]{:S(2)}) %copy-start.4) | copy-done | bytes 49176
  2.9 0.0 copy-start.5
  2.9 0.7 copy-done.5
  3.6 0.0 copy-start.6
  3.6 0.7 copy-done.6
  4.2 66.1 %gather_768.1 = (bf16[768,768]{1,0:T(8,128)(2,1)S(1)}, bf16[768,768]{1,0:T(8,128)(2,1)S(1)}) custom-call(s32[24]{0:T(128)S(1)} %copy-done.6, s32[24,24]{1,0:T(8,128)S(1)} %copy-done.5, bf16[4,6,32,768]{3,2,1,0:T(8,128)(2,1)S(1)} %bitcast.2, bf16[32,768]{1,0:T(8,128)(2,1)S(1)} %copy-done.3, bf16[32,768]{1,0:T(8,128)(2,1)S(1)} %copy-done.4), custom_call_target="tpu_custom_call" | custom-call | tf_op jit(solution)/shard_map/gather_768/pallas_call | solution.py:277
  70.3 0.0 copy-start
  70.3 1.0 %copy-done = bf16[768,768]{1,0:T(8,128)(2,1)} copy-done((bf16[768,768]{1,0:T(8,128)(2,1)}, bf16[768,768]{1,0:T(8,128)(2,1)S(1)}, u32[]{:S(2)}) %copy-start) | copy-done | bytes 1179672
  71.3 0.0 copy-start.1
  71.3 1.0 %copy-done.1 = bf16[768,768]{1,0:T(8,128)(2,1)} copy-done((bf16[768,768]{1,0:T(8,128)(2,1)}, bf16[768,768]{1,0:T(8,128)(2,1)S(1)}, u32[]{:S(2)}) %copy-start.1) | copy-done | bytes 1179672
  72.3 4.3 %second.1 = bf16[768,768]{1,0:T(8,128)(2,1)} custom-call(bf16[768,768]{1,0:T(8,128)(2,1)} %copy-done.1, bf16[768,768]{1,0:T(8,128)(2,1)} %copy-done), custom_call_target="tpu_custom_call" | custom-call | tf_op jit(solution)/shard_map/second/pallas_call | solution.py:306
Async XLA Ops:
  0.0 1.3 %copy-start.2 = (bf16[24,32,768]{2,1,0:T(8,128)(2,1)S(1)}, bf16[24,32,768]{2,1,0:T(8,128)(2,1)}, u32[]{:S(2)}) copy-start(bf16[24,32,768]{2,1,0:T(8,128)(2,1)} %param.5) | copy-start | bytes 3538948
  1.3 0.8 %copy-start.3 = (bf16[32,768]{1,0:T(8,128)(2,1)S(1)}, bf16[32,768]{1,0:T(8,128)(2,1)}, u32[]{:S(2)}) copy-start(bf16[32,768]{1,0:T(8,128)(2,1)} %o_hbm.1) | copy-start | bytes 147460
  2.1 0.8 %copy-start.4 = (bf16[32,768]{1,0:T(8,128)(2,1)S(1)}, bf16[32,768]{1,0:T(8,128)(2,1)}, u32[]{:S(2)}) copy-start(bf16[32,768]{1,0:T(8,128)(2,1)} %v_hbm.1) | copy-start | bytes 147460
  2.9 0.7 copy-start.5
  3.6 0.7 copy-start.6
  70.3 1.0 %copy-start = (bf16[768,768]{1,0:T(8,128)(2,1)}, bf16[768,768]{1,0:T(8,128)(2,1)S(1)}, u32[]{:S(2)}) copy-start(bf16[768,768]{1,0:T(8,128)(2,1)S(1)} %get-tuple-element.8.h_ref) | copy-start | bytes 3538948
  71.3 1.0 %copy-start.1 = (bf16[768,768]{1,0:T(8,128)(2,1)}, bf16[768,768]{1,0:T(8,128)(2,1)S(1)}, u32[]{:S(2)}) copy-start(bf16[768,768]{1,0:T(8,128)(2,1)S(1)} %get-tuple-element.7.v_ref) | copy-start | bytes 3538948

commit v2 on v1

v2 whole, which is shorter than its diff:
```python
import jax
import jax.numpy as jnp
from jax import lax
from jax.experimental import pallas as pl
from jax.experimental.pallas import tpu as pltpu
from jax.sharding import PartitionSpec as P

MESH = pl.DeviceIdType.MESH
NX, NZ, NY = 4, 6, 8
BS, NTILE, NORB = 32, 24, 768
SLABS = NORB // 128
GROUP = NZ * BS
PART = NX * BS


def exchange_kernel(
    fill_hbm, mask_hbm, c_hbm, o_hbm, v_hbm, out_hbm,
    fill_ref, mask_ref, c_in, c_out, c_got, own, full, half_done, done,
    load_sem, send_sem, recv_sem, z_send, z_recv, y_send, y_recv, x_send, x_recv, k_send, k_recv,
):
    row, col, y = lax.axis_index("row"), lax.axis_index("col"), lax.axis_index("ri")
    x, z = col // NZ, col % NZ
    core = row % 2
    other = row + 1 - 2 * core
    half = z // 3

    loads = [
        pltpu.make_async_copy(fill_hbm, fill_ref, load_sem.at[0]),
        pltpu.make_async_copy(mask_hbm, mask_ref, load_sem.at[1]),
        pltpu.make_async_copy(c_hbm, c_in, load_sem.at[2]),
    ]
    for load in loads:
        load.start()

    def load_own(source):
        cols = pl.ds(pl.multiple_of(y * 128, 128), 128)
        return pltpu.make_async_copy(source.at[:, cols], own, load_sem.at[3])

    @pl.when((y < SLABS) & (core == 0))
    def _():
        load_own(o_hbm).start()

    @pl.when((y < SLABS) & (core == 1))
    def _():
        load_own(v_hbm).start()

    barrier = pltpu.get_barrier_semaphore()

    def greet_col(d, _):
        pl.semaphore_signal(barrier, inc=1, device_id={"col": (col + d) % NTILE}, device_id_type=MESH)
        return 0

    def greet_y(d, _):
        pl.semaphore_signal(barrier, inc=1, device_id={"ri": (y + d) % NY}, device_id_type=MESH)
        return 0

    lax.fori_loop(1, NTILE, greet_col, 0)
    lax.fori_loop(1, NY, greet_y, 0)
    pl.semaphore_signal(barrier, inc=1, device_id={"row": other}, device_id_type=MESH)

    loads[0].wait()
    loads[1].wait()
    place = lax.broadcasted_iota(jnp.int32, (8, NORB), 1)
    tile, pos = place // BS, place % BS
    live = jnp.zeros((8, NORB), jnp.int32)
    weight = jnp.zeros((8, NORB), jnp.int32)
    for t in range(NTILE):
        here = (tile == t) & (pos < fill_ref[t])
        live = jnp.where(here, 1, live)
        weight = jnp.where(here, mask_ref[col, t], weight)
    live_cols = live.astype(jnp.float32)[:1]
    live_rows = lax.broadcasted_iota(jnp.int32, (BS, 1), 0) < fill_ref[col]
    screen = (weight.astype(jnp.float32)[:1] * live_rows.astype(jnp.float32)).astype(jnp.bfloat16)

    def out_tile(i):
        turn, odd = i // 2, i % 2
        return (z + turn + odd) % 3 + 3 * ((half + 1 + odd) % 2)

    def in_tile(i):
        turn, odd = i // 2, i % 2
        return (z + 5 - turn + odd) % 3 + 3 * ((half + odd) % 2)

    def pack(i):
        at = out_tile(i)
        c_out[at] = c_in[:, at] * screen[None]

    def z_copy(to, at):
        rows = pl.ds(x * GROUP + at * BS, BS)
        return pltpu.make_async_remote_copy(
            src_ref=own, dst_ref=full.at[core, y, rows],
            send_sem=z_send.at[to], recv_sem=z_recv.at[at],
            device_id={"col": x * NZ + to}, device_id_type=MESH,
        )

    def own_z():
        return pltpu.make_async_copy(own, full.at[core, y, pl.ds(col * BS, BS)], load_sem.at[0])

    def y_copy(to, at):
        rows = pl.ds(x * GROUP, GROUP)
        return pltpu.make_async_remote_copy(
            src_ref=full.at[core, at, rows], dst_ref=full.at[core, at, rows],
            send_sem=y_send.at[to], recv_sem=y_recv.at[at],
            device_id={"ri": to}, device_id_type=MESH,
        )

    def x_copy(to, at, slab):
        rows = pl.ds(at * GROUP, GROUP)
        return pltpu.make_async_remote_copy(
            src_ref=full.at[core, slab, rows], dst_ref=full.at[core, slab, rows],
            send_sem=x_send.at[to, slab], recv_sem=x_recv.at[at, slab],
            device_id={"col": to * NZ + z}, device_id_type=MESH,
        )

    def k_copy(part, at, slab):
        rows = pl.ds(part * GROUP, GROUP)
        return pltpu.make_async_remote_copy(
            src_ref=full.at[at, slab, rows], dst_ref=full.at[at, slab, rows],
            send_sem=k_send.at[part, slab], recv_sem=k_recv.at[part, slab],
            device_id={"row": other}, device_id_type=MESH,
        )

    def slab_at(turn):
        odd = turn % 2
        return (y + odd * (turn + 1) // 2 + (1 - odd) * (NY - turn // 2)) % NY

    def c_copy(to_x, to_z, at_x, at_z):
        return pltpu.make_async_remote_copy(
            src_ref=c_out.at[to_z, to_x], dst_ref=c_got.at[at_z, at_x],
            send_sem=send_sem.at[to_z, to_x], recv_sem=recv_sem.at[at_z, at_x],
            device_id={"col": to_x * NZ + to_z}, device_id_type=MESH,
        )

    def send_tile(i):
        to_z = out_tile(i)

        def send(d, _):
            to_x = (x + d) % NX

            @pl.when((d > 0) | (to_z != z))
            def _():
                c_copy(to_x, to_z, x, z).start()

            return 0

        lax.fori_loop(0, NX, send, 0)

    loads[2].wait()
    lax.fori_loop(0, NZ, lambda i, _: (pack(i), 0)[1], 0)
    pl.semaphore_wait(barrier, NTILE + NY - 1)

    @pl.when(y < SLABS)
    def _():
        def send(d, _):
            z_copy((z + d) % NZ, z).start()
            return 0

        load_own(o_hbm).wait()
        own_z().start()
        lax.fori_loop(1, NZ, send, 0)

    lax.fori_loop(0, NZ, lambda i, _: (send_tile(i), 0)[1], 0)
    keep = pltpu.make_async_copy(c_out.at[z, x], c_got.at[z, x], load_sem.at[1])
    keep.start()

    @pl.when(y < SLABS)
    def _():
        def take(d, _):
            z_copy(z, (z + d) % NZ).wait_recv()
            return 0

        def send(d, _):
            y_copy((y + d) % NY, y).start()
            return 0

        own_z().wait()
        lax.fori_loop(1, NZ, take, 0)
        lax.fori_loop(1, NY, send, 0)

    def spread(turn, _):
        slab = slab_at(turn)

        @pl.when(slab < SLABS)
        def _():
            @pl.when(turn > 0)
            def _():
                y_copy(y, slab).wait_recv()

            def send(d, _):
                x_copy((x + d) % NX, x, slab).start()
                return 0

            lax.fori_loop(1, NX, send, 0)
            k_copy(x, core, slab).start()

        return 0

    lax.fori_loop(0, NY, spread, 0)

    def share(turn, _):
        slab = slab_at(turn)

        @pl.when(slab < SLABS)
        def _():
            def take(d, _):
                part = (x + d) % NX
                x_copy(x, part, slab).wait_recv()
                k_copy(part, core, slab).start()
                return 0

            lax.fori_loop(1, NX, take, 0)

        return 0

    lax.fori_loop(0, NY, share, 0)

    def take_k(which):
        def take(i, _):
            k_copy(i // SLABS, which, i % SLABS).wait_recv()
            return 0

        lax.fori_loop(0, NX * SLABS, take, 0)

    @pl.when(core == 1)
    def _():
        take_k(0)

    occ = jnp.concatenate([full[0, slab] for slab in range(SLABS)], axis=1)
    keep.wait()

    def half_transform(i, _):
        at_z = in_tile(i)

        def take(d, _):
            at_x = (x + d) % NX

            @pl.when((d > 0) | (at_z != z))
            def _():
                c_copy(x, z, at_x, at_z).wait_recv()

            return 0

        lax.fori_loop(0, NX, take, 0)
        got = c_got[at_z].reshape(PART, NORB)
        done = jnp.dot(got, occ, preferred_element_type=jnp.float32).astype(jnp.bfloat16)
        for k in range(NX):
            half_done[pl.ds(k * GROUP + at_z * BS, BS), :] = done[k * BS:(k + 1) * BS]
        return 0

    lax.fori_loop(0, NZ, half_transform, 0)

    @pl.when(core == 0)
    def _():
        take_k(1)

    def store(k):
        rows = pl.ds(k * GROUP, GROUP)
        return pltpu.make_async_copy(done.at[rows], out_hbm.at[rows], load_sem.at[k])

    for k in range(NORB // GROUP):
        rows = pl.ds(k * GROUP, GROUP)
        virt = jnp.concatenate([full[1, slab, rows] for slab in range(SLABS)], axis=1)
        product = jnp.dot(virt, half_done[...], preferred_element_type=jnp.float32) * live_cols
        for t in range(NZ):
            at = lax.broadcasted_iota(jnp.int32, (BS, NORB), 0)
            kept = jnp.where(at < fill_ref[k * NZ + t], product[t * BS:(t + 1) * BS], 0.0)
            done[pl.ds(k * GROUP + t * BS, BS), :] = kept.astype(jnp.bfloat16)
        store(k).start()

    @pl.when(y < SLABS)
    def _():
        def left_z(d, _):
            z_copy((z + d) % NZ, z).wait_send()
            return 0

        def left_y(d, _):
            y_copy((y + d) % NY, y).wait_send()
            return 0

        lax.fori_loop(1, NZ, left_z, 0)
        lax.fori_loop(1, NY, left_y, 0)

    def left_slab(slab, _):
        def left_x(d, _):
            x_copy((x + d) % NX, x, slab).wait_send()
            return 0

        def left_k(part, _):
            k_copy(part, core, slab).wait_send()
            return 0

        lax.fori_loop(1, NX, left_x, 0)
        lax.fori_loop(0, NX, left_k, 0)
        return 0

    def left_c(i, _):
        to_z, to_x = i // NX, i % NX

        @pl.when((to_z != z) | (to_x != x))
        def _():
            c_copy(to_x, to_z, x, z).wait_send()

        return 0

    lax.fori_loop(0, SLABS, left_slab, 0)
    lax.fori_loop(0, NTILE, left_c, 0)
    for k in range(NORB // GROUP):
        store(k).wait()


def exchange(coulomb3, tile_mask, tile_fill, occ_density, virt_density):
    dma = pltpu.SemaphoreType.DMA
    bf16 = jnp.bfloat16
    return pl.pallas_call(
        exchange_kernel,
        out_shape=jax.ShapeDtypeStruct((NORB, NORB), bf16),
        in_specs=[pl.BlockSpec(memory_space=pltpu.HBM)] * 5,
        out_specs=pl.BlockSpec(memory_space=pltpu.HBM),
        scratch_shapes=[
            pltpu.SMEM((NTILE,), jnp.int32),
            pltpu.SMEM((NTILE, NTILE), jnp.int32),
            pltpu.VMEM((NX, NZ, BS, NORB), bf16),
            pltpu.VMEM((NZ, NX, BS, NORB), bf16),
            pltpu.VMEM((NZ, NX, BS, NORB), bf16),
            pltpu.VMEM((BS, 128), bf16),
            pltpu.VMEM((2, SLABS, NORB, 128), bf16),
            pltpu.VMEM((NORB, NORB), bf16),
            pltpu.VMEM((NORB, NORB), bf16),
            dma((5,)), dma((NZ, NX)), dma((NZ, NX)), dma((NZ,)), dma((NZ,)),
            dma((NY,)), dma((NY,)),
            dma((NX, SLABS)), dma((NX, SLABS)), dma((NX, SLABS)), dma((NX, SLABS)),
        ],
        compiler_params=pltpu.CompilerParams(
            collective_id=0, has_side_effects=True, vmem_limit_bytes=60 * 1024 * 1024
        ),
        name="exchange",
    )(tile_fill, tile_mask, coulomb3.reshape(NX, NZ, BS, NORB), occ_density, virt_density)


def on_device(coulomb3, tile_mask, tile_fill, occ_density, virt_density):
    return exchange(coulomb3, tile_mask, tile_fill, occ_density, virt_density)[None, None]


def solution(mesh):
    placed = (P(("row", "ri"), "col", None), P(), P(), P("col", None), P("col", None))
    return jax.shard_map(
        on_device,
        mesh=mesh,
        in_specs=placed,
        out_specs=P(("row", "ri"), "col", None, None),
        check_vma=False,
    )
```

time: 77 us -> 62.3 us (0.81)
  the two profiles are of different devices: /device:TPU:133 before, /device:TPU:159 now
where the time goes in v2:
time: 62.3 us; the launch traced here: 62.1 us
  Pallas kernels  59.7 us (96%)
  local copies, waits for them, and re-layouts  2.36 us (4%)
    pallas_call x1, Pallas kernels, exchange(): pl.pallas_call(exchange_kernel, out_shape=jax.ShapeDtypeStruct((NORB, NOR...  59.7 us
    unnamed x1, local copies, waits for them, and re-layouts  2.36 us

profile of v2, /device:TPU:159, one launch (start us, length us, event | category | flops | bytes accessed | tf_op | source)
XLA Modules:
  0.0 62.1 jit_solution(17805243550129720303)
XLA Ops:
  0.0 59.7 %exchange.1 = bf16[768,768]{1,0:T(8,128)(2,1)} custom-call(s32[24]{0:T(128)} %fill_hbm.1, s32[24,24]{1,0:T(8,128)} %mask_hbm.1, bf16[4,6,32,768]{3,2,1,0:T(8,128)(2,1)} %bitcast.3, bf16[32,768]{1,0:T(8,128)(2,1)} %o_hbm.1, bf16[32,768]{1,0:T(8,128)(2,1)} %v_hbm.1), custom_call_target="tpu_custom_call" | custom-call | tf_op jit(solution)/shard_map/exchange/pallas_call | solution.py:313
  59.7 2.4 %copy.7 = bf16[1,1,768,768]{3,2,1,0:T(8,128)(2,1)} copy(bf16[1,1,768,768]{3,2,1,0:T(8,128)(2,1)} %bitcast.2) | data formatting | bytes 2359296

commit v3 on v2

--- a/solution.py
+++ b/solution.py
@@ -9,6 +9,7 @@
 NX, NZ, NY = 4, 6, 8
 BS, NTILE, NORB = 32, 24, 768
 SLABS = NORB // 128
+LATE = 4
 GROUP = NZ * BS
 PART = NX * BS
 
@@ -77,7 +78,7 @@
         return (z + turn + odd) % 3 + 3 * ((half + 1 + odd) % 2)
 
     def in_tile(i):
-        turn, odd = i // 2, i % 2
+        turn, odd = i % 3, i // 3
         return (z + 5 - turn + odd) % 3 + 3 * ((half + odd) % 2)
 
     def pack(i):
@@ -103,11 +104,11 @@
             device_id={"ri": to}, device_id_type=MESH,
         )
 
-    def x_copy(to, at, slab):
+    def x_copy(to, at, slab, mark=None):
         rows = pl.ds(at * GROUP, GROUP)
         return pltpu.make_async_remote_copy(
             src_ref=full.at[core, slab, rows], dst_ref=full.at[core, slab, rows],
-            send_sem=x_send.at[to, slab], recv_sem=x_recv.at[at, slab],
+            send_sem=x_send.at[to if mark is None else mark, slab], recv_sem=x_recv.at[at, slab],
             device_id={"col": to * NZ + z}, device_id_type=MESH,
         )
 
@@ -158,7 +159,7 @@
         own_z().start()
         lax.fori_loop(1, NZ, send, 0)
 
-    lax.fori_loop(0, NZ, lambda i, _: (send_tile(i), 0)[1], 0)
+    lax.fori_loop(0, NZ - 1, lambda i, _: (send_tile(jnp.where(i < LATE, i, NZ - 1)), 0)[1], 0)
     keep = pltpu.make_async_copy(c_out.at[z, x], c_got.at[z, x], load_sem.at[1])
     keep.start()
 
@@ -185,33 +186,48 @@
             def _():
                 y_copy(y, slab).wait_recv()
 
-            def send(d, _):
-                x_copy((x + d) % NX, x, slab).start()
-                return 0
-
-            lax.fori_loop(1, NX, send, 0)
+            x_copy((x + 1) % NX, x, slab).start()
+            x_copy((x + 3) % NX, x, slab).start()
             k_copy(x, core, slab).start()
 
         return 0
 
     lax.fori_loop(0, NY, spread, 0)
+    send_tile(LATE)
 
     def share(turn, _):
         slab = slab_at(turn)
 
         @pl.when(slab < SLABS)
         def _():
-            def take(d, _):
-                part = (x + d) % NX
+            even = slab % 2 == 0
+            for part, beyond, forward in (
+                ((x + 3) % NX, (x + 1) % NX, even),
+                ((x + 1) % NX, (x + 3) % NX, jnp.logical_not(even)),
+            ):
                 x_copy(x, part, slab).wait_recv()
+
+                @pl.when(forward)
+                def _():
+                    x_copy(beyond, part, slab, (x + 2) % NX).start()
+
                 k_copy(part, core, slab).start()
-                return 0
-
-            lax.fori_loop(1, NX, take, 0)
+
+        return 0
+
+    def share_far(turn, _):
+        slab = slab_at(turn)
+
+        @pl.when(slab < SLABS)
+        def _():
+            part = (x + 2) % NX
+            x_copy(x, part, slab).wait_recv()
+            k_copy(part, core, slab).start()
 
         return 0
 
     lax.fori_loop(0, NY, share, 0)
+    lax.fori_loop(0, NY, share_far, 0)
 
     def take_k(which):
         def take(i, _):

time: 62.3 us -> 60.3 us (0.968)
  the two profiles are of different devices: /device:TPU:159 before, /device:TPU:85 now
where the time goes in v3:
time: 60.3 us; the launch traced here: 60.2 us
  Pallas kernels  57.8 us (96%)
  local copies, waits for them, and re-layouts  2.36 us (4%)
    pallas_call x1, Pallas kernels, exchange(): pl.pallas_call(exchange_kernel, out_shape=jax.ShapeDtypeStruct((NORB, NOR...  57.8 us
    unnamed x1, local copies, waits for them, and re-layouts  2.36 us

profile of v3, /device:TPU:85, one launch (start us, length us, event | category | flops | bytes accessed | tf_op | source)
XLA Modules:
  0.0 60.2 jit_solution(2103661764654993928)
XLA Ops:
  0.0 57.8 %exchange.1 = bf16[768,768]{1,0:T(8,128)(2,1)} custom-call(s32[24]{0:T(128)} %fill_hbm.1, s32[24,24]{1,0:T(8,128)} %mask_hbm.1, bf16[4,6,32,768]{3,2,1,0:T(8,128)(2,1)} %bitcast.3, bf16[32,768]{1,0:T(8,128)(2,1)} %o_hbm.1, bf16[32,768]{1,0:T(8,128)(2,1)} %v_hbm.1), custom_call_target="tpu_custom_call" | custom-call | tf_op jit(solution)/shard_map/exchange/pallas_call | solution.py:329
  57.8 2.4 %copy.7 = bf16[1,1,768,768]{3,2,1,0:T(8,128)(2,1)} copy(bf16[1,1,768,768]{3,2,1,0:T(8,128)(2,1)} %bitcast.2) | data formatting | bytes 2359296

commit v4 on v3

--- a/solution.py
+++ b/solution.py
@@ -10,6 +10,7 @@
 BS, NTILE, NORB = 32, 24, 768
 SLABS = NORB // 128
 LATE = 4
+BLOCK = 384
 GROUP = NZ * BS
 PART = NX * BS
 
@@ -269,17 +270,17 @@
         take_k(1)
 
     def store(k):
-        rows = pl.ds(k * GROUP, GROUP)
+        rows = pl.ds(k * BLOCK, BLOCK)
         return pltpu.make_async_copy(done.at[rows], out_hbm.at[rows], load_sem.at[k])
 
-    for k in range(NORB // GROUP):
-        rows = pl.ds(k * GROUP, GROUP)
+    for k in range(NORB // BLOCK):
+        rows = pl.ds(k * BLOCK, BLOCK)
         virt = jnp.concatenate([full[1, slab, rows] for slab in range(SLABS)], axis=1)
         product = jnp.dot(virt, half_done[...], preferred_element_type=jnp.float32) * live_cols
-        for t in range(NZ):
+        for t in range(BLOCK // BS):
             at = lax.broadcasted_iota(jnp.int32, (BS, NORB), 0)
-            kept = jnp.where(at < fill_ref[k * NZ + t], product[t * BS:(t + 1) * BS], 0.0)
-            done[pl.ds(k * GROUP + t * BS, BS), :] = kept.astype(jnp.bfloat16)
+            kept = jnp.where(at < fill_ref[k * (BLOCK // BS) + t], product[t * BS:(t + 1) * BS], 0.0)
+            done[pl.ds(k * BLOCK + t * BS, BS), :] = kept.astype(jnp.bfloat16)
         store(k).start()
 
     @pl.when(y < SLABS)
@@ -319,7 +320,7 @@
 
     lax.fori_loop(0, SLABS, left_slab, 0)
     lax.fori_loop(0, NTILE, left_c, 0)
-    for k in range(NORB // GROUP):
+    for k in range(NORB // BLOCK):
         store(k).wait()
 
 

time: 60.3 us -> 60.3 us (level)
  no operation moved by 1% of the time
where the time goes in v4:
time: 60.3 us; the launch traced here: 60.1 us
  Pallas kernels  57.8 us (96%)
  local copies, waits for them, and re-layouts  2.36 us (4%)
    pallas_call x1, Pallas kernels, exchange(): pl.pallas_call(exchange_kernel, out_shape=jax.ShapeDtypeStruct((NORB, NOR...  57.8 us
    unnamed x1, local copies, waits for them, and re-layouts  2.36 us

profile of v4, /device:TPU:85, one launch (start us, length us, event | category | flops | bytes accessed | tf_op | source)
XLA Modules:
  0.0 60.1 jit_solution(4435298380850990260)
XLA Ops:
  0.0 57.8 %exchange.1 = bf16[768,768]{1,0:T(8,128)(2,1)} custom-call(s32[24]{0:T(128)} %fill_hbm.1, s32[24,24]{1,0:T(8,128)} %mask_hbm.1, bf16[4,6,32,768]{3,2,1,0:T(8,128)(2,1)} %bitcast.3, bf16[32,768]{1,0:T(8,128)(2,1)} %o_hbm.1, bf16[32,768]{1,0:T(8,128)(2,1)} %v_hbm.1), custom_call_target="tpu_custom_call" | custom-call | tf_op jit(solution)/shard_map/exchange/pallas_call | solution.py:330
  57.8 2.4 %copy.7 = bf16[1,1,768,768]{3,2,1,0:T(8,128)(2,1)} copy(bf16[1,1,768,768]{3,2,1,0:T(8,128)(2,1)} %bitcast.2) | data formatting | bytes 2359296
